TPU v7x, 512 devices: a whole 4x4x16 slice. The times are simulated.
512 devices in a mesh: wide: 64 (over z, y), col: 8 (over x, core).
Axes of the slice: x: 4, y: 4, z: 16, core: 2. Of those that a mesh axis runs over, the one named last changes fastest.
Arguments:
- inputs: bfloat16 [1024, 6144], P('wide', 'col'), may hold values from -6 to 6
- out_grad: bfloat16 [1024, 6144], P('wide', 'col'), may hold values from -6 to 6
- preact: bfloat16 [1024, 24576], P('col', 'wide'), may hold values from -6 to 6
- w_in: bfloat16 [6144, 24576], P('col', 'wide'), may hold values from -0.078125 to 0.078125
- w_out: bfloat16 [24576, 6144], P('wide', 'col'), may hold values from -0.0390625 to 0.0390625
Outputs:
- in_grad: bfloat16 [1024, 6144], P('wide', 'col')
- w_in_grad: float32 [6144, 24576], P('col', 'wide')
- w_out_grad: float32 [24576, 6144], P('wide', 'col')
All inputs are finite; a program needn't handle non-finite values.
Results may differ from a plain program's by a relative error of at most 0.02.
Values may be sent and summed in bfloat16 or wider, within the bound.
A program may use at most 64 MiB of HBM per device.

v0:
```python
import math

import jax
import jax.numpy as jnp
from jax import lax
from jax.sharding import PartitionSpec as P


def gelu_grad(values):
    normal_cdf = 0.5 * (1.0 + lax.erf(values * (1.0 / math.sqrt(2.0))))
    density = jnp.exp(-0.5 * values * values) * (1.0 / math.sqrt(2.0 * math.pi))
    return normal_cdf + values * density


def body(inputs, out_grad, preact, w_in, w_out):
    grad_full = lax.all_gather(out_grad, "wide", axis=0, tiled=True)
    input_full = lax.all_gather(inputs, "wide", axis=0, tiled=True)
    pre_full = lax.all_gather(preact, "col", axis=0, tiled=True)
    act_full = jax.nn.gelu(pre_full.astype(jnp.float32), approximate=False).astype(jnp.bfloat16)
    row_block = grad_full
    act_grad = lax.psum_scatter(
        lax.dot_general(
            row_block, w_out, (((1,), (1,)), ((), ())), preferred_element_type=jnp.float32
        ).astype(jnp.bfloat16),
        "col",
        scatter_dimension=0,
        tiled=True,
    ).astype(jnp.float32)
    hidden_own = (act_grad * gelu_grad(preact.astype(jnp.float32))).astype(jnp.bfloat16)
    hidden_full = lax.all_gather(hidden_own, "col", axis=0, tiled=True)
    w_out_grad = lax.dot_general(
        act_full, grad_full, (((0,), (0,)), ((), ())), preferred_element_type=jnp.float32
    )
    w_in_grad = lax.dot_general(
        input_full, hidden_full, (((0,), (0,)), ((), ())), preferred_element_type=jnp.float32
    )
    row_block = hidden_full
    in_grad = lax.psum_scatter(
        lax.dot_general(
            row_block, w_in, (((1,), (1,)), ((), ())), preferred_element_type=jnp.float32
        ),
        "wide",
        scatter_dimension=0,
        tiled=True,
    ).astype(jnp.bfloat16)
    return (in_grad, w_in_grad, w_out_grad)


def solution(mesh):
    placed = (
        P("wide", "col"),
        P("wide", "col"),
        P("col", "wide"),
        P("col", "wide"),
        P("wide", "col"),
    )
    return jax.shard_map(
        body,
        mesh=mesh,
        in_specs=placed,
        out_specs=(P("wide", "col"), P("col", "wide"), P("wide", "col")),
        check_vma=False,
    )
```

profile of v0, /device:TPU:1, one launch (start us, length us, event | category | flops | bytes accessed | tf_op | source)
XLA Modules:
  0.0 1032.8 jit_solution(1877333937253686682)
XLA Ops:
  7.2 0.0 copy-start
  7.2 0.0 all-gather.3.cloned.1.call-start
  7.2 0.7 all-gather.3.cloned.1.call-update
  7.9 0.0 copy-start.1
  7.9 0.0 reduce-scatter.3.cloned.1.call-start
  8.0 139.6 %all-gather.3.cloned.1.call-done = bf16[1024,768]{1,0:T(8,128)(2,1)} async-done(((bf16[16,768]{1,0:T(8,128)(2,1)}), bf16[1024,768]{1,0:T(8,128)(2,1)}) %all-gather.3.cloned.1.call-update) | async-done | bytes 1572880 | tf_op jit(solution)/shard_map/all_gather | solution.py:16
  147.6 3.4 convolution_convert_fusion
  151.0 0.0 reduce-scatter.3.cloned.1.call-update
  151.0 0.0 all-gather.5.cloned.1.call-start
  151.0 0.7 all-gather.5.cloned.1.call-update
  151.7 0.0 reduce-scatter.5.cloned.1.call-start
  151.8 41.7 %reduce-scatter.3.cloned.1.call-done = bf16[128,384]{1,0:T(8,128)(2,1)} async-done(((bf16[1024,384]{1,0:T(8,128)(2,1)}), bf16[128,384]{1,0:T(8,128)(2,1)}) %reduce-scatter.3.cloned.1.call-update) | async-done | bytes 98320 | tf_op jit(solution)/shard_map/reduce_scatter | solution.py:21
  193.5 0.0 copy-done.1
  193.5 1.0 fusion.70
  194.5 15.5 %all_gather.13 = bf16[1024,384]{1,0:T(8,128)(2,1)S(1)} all-gather(bf16[128,384]{1,0:T(8,128)(2,1)S(1)} %fusion.70), channel_id=1, replica_groups=mesh['wide'=64,'col'=8] {'col'}, dimensions={0}, use_global_device_ids=true | all-gather | bytes 884736 | tf_op jit(solution)/shard_map/all_gather | solution.py:30
  210.1 0.0 copy-done
  210.1 2.6 fusion.101
  212.7 0.0 copy-start.2
  212.7 0.0 reduce-scatter.5.cloned.1.call-update
  212.7 13.6 %all_gather.15 = bf16[1024,384]{1,0:T(8,128)(2,1)S(1)} all-gather(bf16[128,384]{1,0:T(8,128)(2,1)S(1)} %copy-done.1), channel_id=1, replica_groups=mesh['wide'=64,'col'=8] {'col'}, dimensions={0}, use_global_device_ids=true | all-gather | bytes 884736 | tf_op jit(solution)/shard_map/all_gather | solution.py:18
  226.4 0.0 copy-done.2
  226.4 4.8 fusion.31
  231.2 97.6 %all-gather.5.cloned.1.call-done = bf16[1024,768]{1,0:T(8,128)(2,1)} async-done(((bf16[16,768]{1,0:T(8,128)(2,1)}), bf16[1024,768]{1,0:T(8,128)(2,1)}) %all-gather.5.cloned.1.call-update) | async-done | bytes 1572880 | tf_op jit(solution)/shard_map/all_gather | solution.py:17
  328.8 2.2 convolution_bitcast_fusion
  331.0 1.4 copy.8
  332.4 692.5 %reduce-scatter.5.cloned.1.call-done = f32[16,768]{1,0:T(8,128)} async-done(((f32[1024,768]{1,0:T(8,128)}), f32[16,768]{1,0:T(8,128)}) %reduce-scatter.5.cloned.1.call-update) | async-done | bytes 49168 | tf_op jit(solution)/shard_map/reduce_scatter | solution.py:38
  1024.8 1.4 convert_element_type.25
Async XLA Ops:
  7.2 202.9 %copy-start = (bf16[768,384]{1,0:T(8,128)(2,1)S(1)}, bf16[768,384]{1,0:T(8,128)(2,1)}, u32[]{:S(2)}) copy-start(bf16[768,384]{1,0:T(8,128)(2,1)} %param.8) | copy-start | bytes 1769476
  7.2 140.4 %all-gather.3.cloned.1.call-start = ((), (), s32[]{:S(2)}) async-start(), calls=%async_computation.2 | async-start | bytes 1597440 | tf_op jit(solution)/shard_map/all_gather | solution.py:16
  7.9 185.6 %copy-start.1 = (bf16[128,384]{1,0:T(8,128)(2,1)S(1)}, bf16[128,384]{1,0:T(8,128)(2,1)}, u32[]{:S(2)}) copy-start(bf16[128,384]{1,0:T(8,128)(2,1)} %param.7) | copy-start | bytes 294916
  7.9 185.6 %reduce-scatter.3.cloned.1.call-start = ((), (), s32[]{:S(2)}) async-start(), calls=%async_computation.3 | async-start | bytes 884736 | tf_op jit(solution)/shard_map/reduce_scatter | solution.py:21
  151.0 177.8 %all-gather.5.cloned.1.call-start = ((), (), s32[]{:S(2)}) async-start(), calls=%async_computation.5 | async-start | bytes 1597440 | tf_op jit(solution)/shard_map/all_gather | solution.py:17
  151.7 873.1 %reduce-scatter.5.cloned.1.call-start = ((), (), s32[]{:S(2)}) async-start(), calls=%async_computation.4 | async-start | bytes 3194880 | tf_op jit(solution)/shard_map/reduce_scatter | solution.py:38
  212.7 13.7 %copy-start.2 = (bf16[1024,768]{1,0:T(8,128)(2,1)S(1)}, bf16[1024,768]{1,0:T(8,128)(2,1)}, u32[]{:S(2)}) copy-start(bf16[1024,768]{1,0:T(8,128)(2,1)} %all-gather.3.cloned.1.call-done) | copy-start | bytes 4718596
Sparse Core Ops, SparseCore 0:
  11.0 136.5 all-gather.2
  151.1 42.3 reduce-scatter.2
  196.9 131.8 all-gather.4
  333.6 691.1 reduce-scatter.4
where the time goes:
time: 1040 us; the launch traced here: 1030 us
  waiting for transfers between devices  973 us (94%)
  blocking collectives  29.2 us (3%)
  between operations  13.8 us (1%)
  matrix products  13.1 us (1%)
    reduce_scatter x1, waiting for transfers between devices, body(): lax.psum_scatter(lax.dot_general(row_block, w_in, (((1,), (1,)), ((), ())...  692 us
    all_gather x1, waiting for transfers between devices, body(): grad_full = lax.all_gather(out_grad, 'wide', axis=0, tiled=True)  140 us
    all_gather x1, waiting for transfers between devices, body(): input_full = lax.all_gather(inputs, 'wide', axis=0, tiled=True)  97.6 us
    reduce_scatter x1, waiting for transfers between devices, body(): lax.psum_scatter(lax.dot_general(row_block, w_out, (((1,), (1,)), ((), ()...  41.7 us
  transfers between devices with their start and end apart: 4, of which 4 were waited for; matrix products, arithmetic and copies ran while one was open for 1% of the time, Pallas kernels for 0%

commit v1 on v0

v1 whole, which is shorter than its diff:
```python
import functools
import math

import jax
import jax.numpy as jnp
from jax import lax
from jax.experimental import pallas as pl
from jax.experimental.pallas import tpu as pltpu
from jax.sharding import PartitionSpec as P

MESH = pl.DeviceIdType.MESH
NZ, NY, NC = 16, 4, 8
ROWS = 16
STAGES = 4
BF16, F32 = jnp.bfloat16, jnp.float32


def normal_cdf(values):
    return 0.5 * (1.0 + lax.erf(values * (1.0 / math.sqrt(2.0))))


def gelu_grad(values):
    density = jnp.exp(-0.5 * values * values) * (1.0 / math.sqrt(2.0 * math.pi))
    return normal_cdf(values) + values * density


def dot(a, b, contract):
    return lax.dot_general(a, b, (contract, ((), ())), preferred_element_type=F32)


def stage_offset(stage, quarter):
    return -(2 * stage + 1) + quarter % 2 + (4 * stage + 2) * (quarter // 2)


def slot_of(offset):
    return offset + 7


def back(offset):
    return 8 if offset == 8 else -offset


def kernel(
    grad_hbm, inp_hbm, pre_hbm, w_in_hbm, w_out_hbm,
    in_grad_ref, w_in_grad_hbm, w_out_grad_hbm,
    g, inp, pre, act, hid, w_in, w_out, xs, xr, part, ys, yr, zs, zr, wig, wog,
    local_sem,
    gz_s, gz_r, gy_s, gy_r, pre_s, pre_r, x_s, x_r, h_s, h_r, y_s, y_r, z_s, z_r, iy_s, iy_r, iz_s, iz_r,
):
    wide, col = lax.axis_index("wide"), lax.axis_index("col")
    z, y = wide // NY, wide % NY

    def at_z(offset):
        return (z + offset + NZ) % NZ

    def at_y(offset):
        return (y + offset) % NY

    def dev_z(offset):
        return (at_z(offset) * NY + y, col)

    def dev_y(offset):
        return (z * NY + at_y(offset), col)

    def dev_c(offset):
        return (wide, (col + offset) % NC)

    sends = []

    def send(src, dst, send_sem, recv_sem, device):
        copy = pltpu.make_async_remote_copy(
            src_ref=src, dst_ref=dst, send_sem=send_sem, recv_sem=recv_sem, device_id=device, device_id_type=MESH
        )
        copy.start()
        sends.append(copy)

    def arrived(dst, send_sem, recv_sem):
        pltpu.make_async_remote_copy(
            src_ref=dst, dst_ref=dst, send_sem=send_sem, recv_sem=recv_sem, device_id=dev_y(1), device_id_type=MESH
        ).wait_recv()

    loads = [
        pltpu.make_async_copy(grad_hbm, g.at[z, y], local_sem.at[0]),
        pltpu.make_async_copy(pre_hbm, pre.at[pl.ds(2 * col, 2)], local_sem.at[1]),
        pltpu.make_async_copy(inp_hbm, inp.at[z, y], local_sem.at[2]),
        pltpu.make_async_copy(w_out_hbm, w_out, local_sem.at[3]),
        pltpu.make_async_copy(w_in_hbm, w_in, local_sem.at[4]),
    ]
    for load in loads:
        load.start()

    barrier = pltpu.get_barrier_semaphore()
    partners = [dev_z(d) for d in (1, -1, 2, -2)] + [dev_y(d) for d in (1, 2, 3)] + [dev_c(d) for d in range(1, NC)]
    for partner in partners:
        pl.semaphore_signal(barrier, inc=1, device_id=partner, device_id_type=MESH)
    pl.semaphore_wait(barrier, len(partners))

    def z_pass(offset, hop):
        seen = offset - hop
        block = g.at[at_z(offset), y]
        send(block, block, gz_s.at[slot_of(seen)], gz_r.at[slot_of(seen)], dev_z(hop))

    def z_wait(offset):
        arrived(g.at[at_z(offset), y], gz_s.at[slot_of(offset)], gz_r.at[slot_of(offset)])

    def y_pass(offset):
        block = g.at[at_z(offset), y]
        for d in (1, 2, 3):
            send(block, block, gy_s.at[slot_of(offset), d - 1], gy_r.at[slot_of(offset), d - 1], dev_y(d))

    def y_wait(offset):
        for d in (1, 2, 3):
            arrived(
                g.at[at_z(offset), at_y(NY - d)], gy_s.at[slot_of(offset), d - 1], gy_r.at[slot_of(offset), d - 1]
            )

    def gather_step(step):
        far, near = 2 * step + 2, 2 * step + 1
        z_wait(far)
        if step < 3:
            z_pass(far, -2)
            z_pass(far, -1)
            z_wait(-far)
            if step < 2:
                z_pass(-far, 2)
            z_pass(-far, 1)
        y_pass(far)
        if step < 3:
            y_pass(-far)
        z_wait(near)
        y_pass(near)
        z_wait(-near)
        y_pass(-near)

    def inputs_over_y():
        block = inp.at[z, y]
        for d in (1, 2, 3):
            send(block, block, iy_s.at[d - 1], iy_r.at[d - 1], dev_y(d))

    def inputs_step(step):
        if step == 0:
            for d in (1, 2, 3):
                arrived(inp.at[z, at_y(NY - d)], iy_s.at[d - 1], iy_r.at[d - 1])
        for way in (1, -1):
            offset = way * step
            if step and offset != -8:
                arrived(inp.at[at_z(offset)], iz_s.at[slot_of(offset)], iz_r.at[slot_of(offset)])
            seen = offset + way
            if step < 8 and seen != -8:
                block = inp.at[at_z(offset)]
                send(block, block, iz_s.at[slot_of(seen)], iz_r.at[slot_of(seen)], dev_z(-way))

    def gelu_chunk(index):
        values = pre[pl.ds(2 * index, 2)].astype(F32)
        act[pl.ds(2 * index, 2)] = (values * normal_cdf(values)).astype(BF16)

    def stage_blocks(stage):
        return [at_z(stage_offset(stage, quarter)) for quarter in range(4)]

    def stage_rows(ref, stage):
        return jnp.concatenate([ref[b].reshape(NY * ROWS, ref.shape[-1]) for b in stage_blocks(stage)], axis=0)

    own_block = [at_z(stage_offset(stage, col // 2)) for stage in range(STAGES)]
    own_half = pl.ds(2 * (col % 2), 2)

    def phase_b(stage):
        for quarter in range(4):
            y_wait_offset = stage_offset(stage, quarter)
            y_wait(y_wait_offset)
        partial = dot(stage_rows(g, stage), w_out[...], ((1,), (1,))).astype(BF16)
        xs[stage] = partial.reshape(NC, 2, ROWS, partial.shape[-1])
        for r in range(1, NC):
            send(xs.at[stage, (col + r) % NC], xr.at[stage, r], x_s.at[stage, r], x_r.at[stage, r], dev_c(r))

    def phase_c(stage):
        total = xs[stage, col].astype(F32)
        for r in range(1, NC):
            arrived(xr.at[stage, r], x_s.at[stage, r], x_r.at[stage, r])
            total = total + xr[stage, r].astype(F32)
        block = own_block[stage]
        own = pre[block, own_half].astype(F32)
        hid[block, own_half] = (total * gelu_grad(own)).astype(BF16)
        piece = hid.at[block, own_half]
        for r in range(1, NC):
            send(piece, piece, h_s.at[stage, r], h_r.at[stage, r], dev_c(r))

    def phase_d(stage):
        for r in range(1, NC):
            source = (col + NC - r) % NC
            piece = hid.at[at_z(stage_offset(stage, source // 2)), pl.ds(2 * (source % 2), 2)]
            arrived(piece, h_s.at[stage, r], h_r.at[stage, r])
        partial = dot(stage_rows(hid, stage), w_in[...], ((1,), (1,)))
        part[stage] = partial.reshape(4, NY, ROWS, partial.shape[-1])
        for d in (2, 1, 3):
            ys[stage, d - 1] = part[stage, :, at_y(d)].astype(BF16)
            send(ys.at[stage, d - 1], yr.at[stage, d - 1], y_s.at[stage, d - 1], y_r.at[stage, d - 1], dev_y(d))

    def phase_e(stage):
        for d in (1, 2, 3):
            arrived(yr.at[stage, d - 1], y_s.at[stage, d - 1], y_r.at[stage, d - 1])
        for quarter in (3, 0, 2, 1):
            offset = stage_offset(stage, quarter)
            total = part[stage, quarter, y]
            for d in (1, 2, 3):
                total = total + yr[stage, d - 1, quarter].astype(F32)
            seen = slot_of(back(offset))
            zs[seen] = total.astype(BF16)
            if offset:
                send(zs.at[seen], zr.at[seen], z_s.at[seen], z_r.at[seen], dev_z(offset))

    loads[0].wait()
    for hop in (2, -2, 1, -1):
        z_pass(0, hop)
    y_pass(0)
    loads[1].wait()
    own_pre = pre.at[pl.ds(2 * col, 2)]
    for r in range(1, NC):
        send(own_pre, own_pre, pre_s.at[r], pre_r.at[r], dev_c(r))
    loads[2].wait()
    inputs_over_y()
    loads[3].wait()
    loads[4].wait()

    stores = []
    for it in range(2 * STAGES):
        if it < STAGES:
            gather_step(it)
        inputs_step(it)
        for phase, lag in ((phase_b, 1), (phase_c, 2), (phase_d, 3), (phase_e, 4)):
            if 0 <= it - lag < STAGES:
                phase(it - lag)
        if it == 0:
            for r in range(1, NC):
                arrived(pre.at[pl.ds(2 * ((col + NC - r) % NC), 2)], pre_s.at[r], pre_r.at[r])
        if it < 4:
            gelu_chunk(2 * it)
            gelu_chunk(2 * it + 1)
        if it == 4:
            wog[...] = dot(
                act[...].reshape(NZ * NY * ROWS, act.shape[-1]), g[...].reshape(NZ * NY * ROWS, g.shape[-1]), ((0,), (0,))
            )
            store = pltpu.make_async_copy(wog, w_out_grad_hbm, local_sem.at[5])
            store.start()
            stores.append(store)
    inputs_step(8)
    wig[...] = dot(
        inp[...].reshape(NZ * NY * ROWS, inp.shape[-1]), hid[...].reshape(NZ * NY * ROWS, hid.shape[-1]), ((0,), (0,))
    )
    store = pltpu.make_async_copy(wig, w_in_grad_hbm, local_sem.at[6])
    store.start()
    stores.append(store)

    total = zs[slot_of(0)].astype(F32)
    for offset in (1, -1, 2, -2, 3, -3, 4, -4, 5, -5, 6, -6, 7, -7, 8):
        seen = slot_of(offset)
        arrived(zr.at[seen], z_s.at[seen], z_r.at[seen])
        total = total + zr[seen].astype(F32)
    in_grad_ref[...] = total.astype(BF16)
    for copy in sends:
        copy.wait_send()
    for store in stores:
        store.wait()


def body(inputs, out_grad, preact, w_in, w_out):
    width, hidden = w_in.shape
    dma = pltpu.SemaphoreType.DMA
    any_space = pl.BlockSpec(memory_space=pl.ANY)
    pairs = [(16,), (16, 3), (NC,), (STAGES, NC), (STAGES, NC), (STAGES, 3), (16,), (3,), (16,)]
    return pl.pallas_call(
        kernel,
        name="mlp_backward",
        out_shape=(
            jax.ShapeDtypeStruct((ROWS, width), BF16),
            jax.ShapeDtypeStruct((width, hidden), F32),
            jax.ShapeDtypeStruct((hidden, width), F32),
        ),
        in_specs=[any_space] * 5,
        out_specs=(pl.BlockSpec(memory_space=pltpu.VMEM), any_space, any_space),
        scratch_shapes=[
            pltpu.VMEM((NZ, NY, ROWS, width), BF16),
            pltpu.VMEM((NZ, NY, ROWS, width), BF16),
            pltpu.VMEM((NZ, NY, ROWS, hidden), BF16),
            pltpu.VMEM((NZ, NY, ROWS, hidden), BF16),
            pltpu.VMEM((NZ, NY, ROWS, hidden), BF16),
            pltpu.VMEM((width, hidden), BF16),
            pltpu.VMEM((hidden, width), BF16),
            pltpu.VMEM((STAGES, NC, 2, ROWS, hidden), BF16),
            pltpu.VMEM((STAGES, NC, 2, ROWS, hidden), BF16),
            pltpu.VMEM((STAGES, 4, NY, ROWS, width), F32),
            pltpu.VMEM((STAGES, 3, 4, ROWS, width), BF16),
            pltpu.VMEM((STAGES, 3, 4, ROWS, width), BF16),
            pltpu.VMEM((16, ROWS, width), BF16),
            pltpu.VMEM((16, ROWS, width), BF16),
            pltpu.VMEM((width, hidden), F32),
            pltpu.VMEM((hidden, width), F32),
            dma((7,)),
        ]
        + [dma(shape) for shape in pairs for _ in range(2)],
        compiler_params=pltpu.CompilerParams(collective_id=0, has_side_effects=True, vmem_limit_bytes=48 << 20),
    )(out_grad, inputs, preact.reshape(2, NY, ROWS, hidden), w_in, w_out)


def solution(mesh):
    placed = (
        P("wide", "col"),
        P("wide", "col"),
        P("col", "wide"),
        P("col", "wide"),
        P("wide", "col"),
    )
    return jax.shard_map(
        body,
        mesh=mesh,
        in_specs=placed,
        out_specs=(P("wide", "col"), P("col", "wide"), P("wide", "col")),
        check_vma=False,
    )
```

time: 1040 us -> 86.1 us (0.08)
  the two profiles are of different devices: /device:TPU:1 before, /device:TPU:40 now
where the time goes in v1:
time: 86.1 us; the launch traced here: 85.7 us
  Pallas kernels  77.9 us (90%)
  local copies, waits for them, and re-layouts  7.12 us (8%)
    pallas_call x1, Pallas kernels, body(): pl.pallas_call(kernel, name='mlp_backward', out_shape=(jax.ShapeDtypeStru...  77.9 us
    unnamed x13, local copies, waits for them, and re-layouts  7.12 us

profile of v1, /device:TPU:40, one launch (start us, length us, event | category | flops | bytes accessed | tf_op | source)
XLA Modules:
  0.0 85.7 jit_solution(12393695088815995753)
XLA Ops:
  0.6 0.0 copy-start
  0.6 1.1 %copy-done = bf16[768,384]{1,0:T(8,128)(2,1)S(1)} copy-done((bf16[768,384]{1,0:T(8,128)(2,1)S(1)}, bf16[768,384]{1,0:T(8,128)(2,1)}, u32[]{:S(2)}) %copy-start) | copy-done | bytes 589848
  1.7 0.0 copy-start.1
  1.7 1.1 %copy-done.1 = bf16[384,768]{1,0:T(8,128)(2,1)S(1)} copy-done((bf16[384,768]{1,0:T(8,128)(2,1)S(1)}, bf16[384,768]{1,0:T(8,128)(2,1)}, u32[]{:S(2)}) %copy-start.1) | copy-done | bytes 589848
  2.8 0.0 copy-start.2
  2.8 0.9 %copy-done.2 = bf16[128,384]{1,0:T(8,128)(2,1)S(1)} copy-done((bf16[128,384]{1,0:T(8,128)(2,1)S(1)}, bf16[128,384]{1,0:T(8,128)(2,1)}, u32[]{:S(2)}) %copy-start.2) | copy-done | bytes 98328
  3.7 0.0 copy-start.3
  3.7 0.7 copy-done.3
  4.4 0.0 copy-start.4
  4.4 0.7 copy-done.4
  5.1 77.9 %mlp_backward.1 = (bf16[16,768]{1,0:T(8,128)(2,1)S(1)}, f32[768,384]{1,0:T(8,128)S(1)}, f32[384,768]{1,0:T(8,128)S(1)}) custom-call(bf16[16,768]{1,0:T(8,128)(2,1)S(1)} %copy-done.3, bf16[16,768]{1,0:T(8,128)(2,1)S(1)} %copy-done.4, bf16[2,4,16,384]{3,2,1,0:T(8,128)(2,1)S(1)} %bitcast.1, bf16[768,384]{1,0:T(8,128)(2,1)S(1)} %copy-done, ...), custom_call_target="tpu_custom_call" | custom-call | tf_op jit(solution)/shard_map/mlp_backward/pallas_call | solution.py:270
  83.1 0.6 copy.11
  83.7 1.0 %copy.12 = f32[768,384]{1,0:T(8,128)} copy(f32[768,384]{1,0:T(8,128)S(1)} %get-tuple-element.7) | data formatting | bytes 2359296
  84.7 1.0 %copy.13 = f32[384,768]{1,0:T(8,128)} copy(f32[384,768]{1,0:T(8,128)S(1)} %get-tuple-element.8) | data formatting | bytes 2359296
Async XLA Ops:
  0.6 1.1 %copy-start = (bf16[768,384]{1,0:T(8,128)(2,1)S(1)}, bf16[768,384]{1,0:T(8,128)(2,1)}, u32[]{:S(2)}) copy-start(bf16[768,384]{1,0:T(8,128)(2,1)} %w_in_hbm.1) | copy-start | bytes 1769476
  1.7 1.1 %copy-start.1 = (bf16[384,768]{1,0:T(8,128)(2,1)S(1)}, bf16[384,768]{1,0:T(8,128)(2,1)}, u32[]{:S(2)}) copy-start(bf16[384,768]{1,0:T(8,128)(2,1)} %w_out_hbm.1) | copy-start | bytes 1769476
  2.8 0.9 %copy-start.2 = (bf16[128,384]{1,0:T(8,128)(2,1)S(1)}, bf16[128,384]{1,0:T(8,128)(2,1)}, u32[]{:S(2)}) copy-start(bf16[128,384]{1,0:T(8,128)(2,1)} %param.7) | copy-start | bytes 294916
  3.7 0.7 copy-start.3
  4.4 0.7 copy-start.4

commit v2 on v1

v2 whole, which is shorter than its diff:
```python
import functools
import math

import jax
import jax.numpy as jnp
from jax import lax
from jax.experimental import pallas as pl
from jax.experimental.pallas import tpu as pltpu
from jax.sharding import PartitionSpec as P

MESH = pl.DeviceIdType.MESH
NZ, NY, NC = 16, 4, 8
ROWS = 16
HEAD = 256
INP_HEAD = 256
INP_REACH = 2
STAGES = 4
BF16, F32 = jnp.bfloat16, jnp.float32


def normal_cdf(values):
    return 0.5 * (1.0 + lax.erf(values * (1.0 / math.sqrt(2.0))))


def gelu_grad(values):
    density = jnp.exp(-0.5 * values * values) * (1.0 / math.sqrt(2.0 * math.pi))
    return normal_cdf(values) + values * density


def dot(a, b, contract):
    return lax.dot_general(a, b, (contract, ((), ())), preferred_element_type=F32)


def stage_offset(stage, quarter):
    return -(2 * stage + 1) + quarter % 2 + (4 * stage + 2) * (quarter // 2)


def slot_of(offset):
    return offset + 7


def back(offset):
    return 8 if offset == 8 else -offset


def kernel(
    grad_hbm, inp_hbm, pre_hbm, w_in_hbm, w_out_hbm,
    in_grad_ref, wig, wog,
    ga, gb, ia, ib, pre, act, hid, w_in, w_out, xs, xr, part, ys, yr, zs, zr,
    local_sem,
    grad_sems, inp_sems, pre_s, pre_r, x_s, x_r, h_s, h_r, y_s, y_r, z_s, z_r,
):
    wide, col = lax.axis_index("wide"), lax.axis_index("col")
    z, y, x, core = wide // NY, wide % NY, col // 2, col % 2

    def at_z(offset):
        return (z + offset + NZ) % NZ

    def at_y(offset):
        return (y + offset) % NY

    def dev_z(offset):
        return (at_z(offset) * NY + y, col)

    def dev_y(offset):
        return (z * NY + at_y(offset), col)

    col_offsets = (4, 5, 2, 3, 6, 7, 1)

    def other_col(offset):
        return 2 * ((x + offset // 2) % 4) + (core + offset) % 2

    def dev_c(offset):
        return (wide, other_col(offset))

    def source_col(offset):
        return 2 * ((x + 4 - offset // 2) % 4) + (core + offset) % 2

    sends = []

    def send(src, dst, send_sem, recv_sem, device):
        copy = pltpu.make_async_remote_copy(
            src_ref=src, dst_ref=dst, send_sem=send_sem, recv_sem=recv_sem, device_id=device, device_id_type=MESH
        )
        copy.start()
        sends.append(copy)

    def arrived(dst, send_sem, recv_sem):
        pltpu.make_async_remote_copy(
            src_ref=dst, dst_ref=dst, send_sem=send_sem, recv_sem=recv_sem, device_id=dev_y(1), device_id_type=MESH
        ).wait_recv()

    def local(src, dst, index):
        copy = pltpu.make_async_copy(src, dst, local_sem.at[index])
        copy.start()
        return copy

    grad_loads = [
        local(grad_hbm.at[:, HEAD:], gb.at[z, y], 0),
        local(grad_hbm.at[:, :HEAD], ga.at[z, y], 1),
    ]
    pre_load = local(pre_hbm, pre.at[pl.ds(2 * col, 2)], 2)
    inp_loads = [local(inp_hbm.at[:, INP_HEAD:], ib.at[z, y], 3)] if INP_HEAD < inp_hbm.shape[1] else []
    inp_loads.append(local(inp_hbm.at[:, :INP_HEAD], ia.at[z, y], 6))

    barrier = pltpu.get_barrier_semaphore()
    greeted = [dev_z(d) for d in (1, -1, 2, -2)] + [dev_y(d) for d in (1, 2, 3)] + [dev_c(r) for r in col_offsets]
    for other in greeted:
        pl.semaphore_signal(barrier, inc=1, device_id=other, device_id_type=MESH)
    pl.semaphore_wait(barrier, len(greeted))

    def gather(head, rest, sems, reach):
        hy_s, hy_r, hz_s, hz_r, rz_s, rz_r, ry_s, ry_r = sems

        def head_block(offset):
            return head.at[at_z(offset)], hz_s, hz_r

        def rest_block(offset):
            return rest.at[at_z(offset), y], rz_s, rz_r

        def z_pass(part, offset, hop):
            seen = slot_of(offset - hop)
            block, send_sem, recv_sem = part(offset)
            send(block, block, send_sem.at[seen], recv_sem.at[seen], dev_z(hop))

        def z_wait(part, offset):
            block, send_sem, recv_sem = part(offset)
            arrived(block, send_sem.at[slot_of(offset)], recv_sem.at[slot_of(offset)])

        def y_pass(offset):
            block = rest.at[at_z(offset), y]
            for d in (1, 3, 2):
                slot = NY * slot_of(offset) + d
                send(block, block, ry_s.at[slot], ry_r.at[slot], dev_y(d))

        def y_wait(offset):
            for d in (1, 2, 3):
                slot = NY * slot_of(offset) + d
                arrived(rest.at[at_z(offset), at_y(NY - d)], ry_s.at[slot], ry_r.at[slot])

        def z_start(part):
            for hop in range(reach, 0, -1):
                z_pass(part, 0, hop)
                z_pass(part, 0, -hop)

        def z_step(part, step, then):
            waiting = []
            for back_off in range(reach):
                for way in (1, -1):
                    offset = way * (reach * step - back_off)
                    if offset == -8:
                        continue
                    z_wait(part, offset)
                    if back_off == 0 and reach * step < 8:
                        for hop in range(reach, 0, -1):
                            if offset + hop * way != -8:
                                z_pass(part, offset, -hop * way)
                    waiting.append(offset)
                    if back_off or way < 0 or reach * step == 8:
                        for passed in waiting:
                            then(passed)
                        waiting = []

        def start():
            if rest is not None:
                z_start(rest_block)
            block = head.at[z, y]
            for d in (1, 3, 2):
                send(block, block, hy_s.at[d], hy_r.at[d], dev_y(d))
            if rest is not None:
                y_pass(0)

        def rest_step(step):
            z_step(rest_block, step, y_pass)

        def head_step(step):
            if step == 0:
                for d in (1, 2, 3):
                    arrived(head.at[z, at_y(NY - d)], hy_s.at[d], hy_r.at[d])
                z_start(head_block)
            else:
                z_step(head_block, step, lambda offset: None)

        return start, rest_step, head_step, y_wait

    grad_start, grad_rest, grad_head, grad_wait = gather(ga, gb, grad_sems, 2)
    inp_start, inp_rest, inp_head, inp_wait = gather(ia, ib, inp_sems, INP_REACH)

    def flat(ref):
        return ref[...].reshape(NZ * NY * ROWS, ref.shape[-1])

    def gelu_chunk(index):
        values = pre[pl.ds(2 * index, 2)].astype(F32)
        act[pl.ds(2 * index, 2)] = (values * normal_cdf(values)).astype(BF16)

    def stage_blocks(stage):
        return [at_z(stage_offset(stage, quarter)) for quarter in range(4)]

    def stage_rows(ref, stage):
        return jnp.concatenate([ref[b].reshape(NY * ROWS, ref.shape[-1]) for b in stage_blocks(stage)], axis=0)

    own_block = [at_z(stage_offset(stage, col // 2)) for stage in range(STAGES)]
    own_half = pl.ds(2 * (col % 2), 2)

    def phase_b(stage):
        for quarter in range(4):
            grad_wait(stage_offset(stage, quarter))
        partial = dot(stage_rows(ga, stage), w_out[:, :HEAD], ((1,), (1,)))
        partial = (partial + dot(stage_rows(gb, stage), w_out[:, HEAD:], ((1,), (1,)))).astype(BF16)
        xs[stage] = partial.reshape(NC, 2, ROWS, partial.shape[-1])
        for r in col_offsets:
            send(xs.at[stage, other_col(r)], xr.at[stage, r], x_s.at[stage, r], x_r.at[stage, r], dev_c(r))

    def phase_c(stage):
        total = xs[stage, col].astype(F32)
        for r in col_offsets[::-1]:
            arrived(xr.at[stage, r], x_s.at[stage, r], x_r.at[stage, r])
            total = total + xr[stage, r].astype(F32)
        block = own_block[stage]
        own = pre[block, own_half].astype(F32)
        hid[block, own_half] = (total * gelu_grad(own)).astype(BF16)
        piece = hid.at[block, own_half]
        for r in col_offsets:
            send(piece, piece, h_s.at[stage, r], h_r.at[stage, r], dev_c(r))

    def phase_d(stage):
        for r in col_offsets[::-1]:
            source = source_col(r)
            piece = hid.at[at_z(stage_offset(stage, source // 2)), pl.ds(2 * (source % 2), 2)]
            arrived(piece, h_s.at[stage, r], h_r.at[stage, r])
        partial = dot(stage_rows(hid, stage), w_in[...], ((1,), (1,)))
        part[stage] = partial.reshape(4, NY, ROWS, partial.shape[-1])
        for quarter in (3, 0, 2, 1):
            for d in (2, 1, 3):
                slot = NY * quarter + d
                ys[stage, slot] = part[stage, quarter, at_y(d)].astype(BF16)
                send(ys.at[stage, slot], yr.at[stage, slot], y_s.at[stage, slot], y_r.at[stage, slot], dev_y(d))

    def phase_e(stage):
        for quarter in (3, 0, 2, 1):
            offset = stage_offset(stage, quarter)
            total = part[stage, quarter, y]
            for d in (1, 3, 2):
                slot = NY * quarter + d
                arrived(yr.at[stage, slot], y_s.at[stage, slot], y_r.at[stage, slot])
                total = total + yr[stage, slot].astype(F32)
            seen = slot_of(back(offset))
            zs[seen] = total.astype(BF16)
            if offset:
                send(zs.at[seen], zr.at[seen], z_s.at[seen], z_r.at[seen], dev_z(offset))

    for load in grad_loads:
        load.wait()
    grad_start()
    pre_load.wait()
    own_pre = pre.at[pl.ds(2 * col, 2)]
    for r in col_offsets:
        send(own_pre, own_pre, pre_s.at[r], pre_r.at[r], dev_c(r))
    weight_loads = [local(w_out_hbm, w_out, 4), local(w_in_hbm, w_in, 5)]

    def start_inputs():
        for load in inp_loads:
            load.wait()
        inp_start()

    def wait_preact():
        for r in col_offsets:
            arrived(pre.at[pl.ds(2 * source_col(r), 2)], pre_s.at[r], pre_r.at[r])

    def wait_weights():
        for load in weight_loads:
            load.wait()

    def gelu_part(index):
        gelu_chunk(2 * index)
        gelu_chunk(2 * index + 1)

    def w_out_grad():
        for gathered, columns in ((ga, slice(0, HEAD)), (gb, slice(HEAD, None))):
            wog[:, columns] = dot(flat(act), flat(gathered), ((0,), (0,)))

    def w_in_grad():
        if ib is not None:
            for offset in range(-7, 9):
                inp_wait(offset)
            wig[INP_HEAD:] = dot(flat(ib), flat(hid), ((0,), (0,)))
        wig[:INP_HEAD] = dot(flat(ia), flat(hid), ((0,), (0,)))

    for step, *index in (
        (grad_rest, 1), (grad_head, 0), (wait_weights,), (start_inputs,), (grad_rest, 2), (grad_head, 1),
        (inp_rest, 1), (inp_head, 0), (phase_b, 0), (wait_preact,), (gelu_part, 0), (gelu_part, 1), (grad_rest, 3),
        (grad_head, 2), (inp_rest, 2), (inp_head, 1), (phase_b, 1), (phase_c, 0), (gelu_part, 2), (gelu_part, 3),
        (grad_rest, 4), (grad_head, 3), (inp_rest, 3), (inp_head, 2), (phase_b, 2), (phase_c, 1), (phase_d, 0),
        (grad_head, 4), (phase_b, 3), (inp_rest, 4), (inp_head, 3), (phase_c, 2), (phase_d, 1), (phase_e, 0),
        (w_out_grad,), (phase_c, 3), (inp_head, 4), (phase_d, 2), (phase_e, 1), (phase_d, 3), (phase_e, 2),
        (phase_e, 3), (w_in_grad,),
    ):
        step(*index)

    total = zs[slot_of(0)].astype(F32)
    for offset in (1, -1, 2, -2, 3, -3, 4, -4, 5, -5, 6, -6, 7, -7, 8):
        seen = slot_of(offset)
        arrived(zr.at[seen], z_s.at[seen], z_r.at[seen])
        total = total + zr[seen].astype(F32)
    in_grad_ref[...] = total.astype(BF16)
    for copy in sends:
        copy.wait_send()


def body(inputs, out_grad, preact, w_in, w_out):
    width, hidden = w_in.shape
    dma = pltpu.SemaphoreType.DMA
    any_space = pl.BlockSpec(memory_space=pl.ANY)
    gather_sems = [dma((size,)) for size in (NY, NY, 16, 16, 16, 16, 16 * NY, 16 * NY)]
    pairs = [(NC,), (STAGES, NC), (STAGES, NC), (STAGES, 4 * NY), (16,)]
    return pl.pallas_call(
        kernel,
        name="mlp_backward",
        out_shape=(
            pltpu.VMEM((ROWS, width), BF16),
            pltpu.VMEM((width, hidden), F32),
            pltpu.VMEM((hidden, width), F32),
        ),
        in_specs=[any_space] * 5,
        out_specs=(pl.BlockSpec(memory_space=pltpu.VMEM),) * 3,
        scratch_shapes=[
            pltpu.VMEM((NZ, NY, ROWS, HEAD), BF16),
            pltpu.VMEM((NZ, NY, ROWS, width - HEAD), BF16),
            pltpu.VMEM((NZ, NY, ROWS, INP_HEAD), BF16),
            pltpu.VMEM((NZ, NY, ROWS, width - INP_HEAD), BF16) if INP_HEAD < width else None,
            pltpu.VMEM((NZ, NY, ROWS, hidden), BF16),
            pltpu.VMEM((NZ, NY, ROWS, hidden), BF16),
            pltpu.VMEM((NZ, NY, ROWS, hidden), BF16),
            pltpu.VMEM((width, hidden), BF16),
            pltpu.VMEM((hidden, width), BF16),
            pltpu.VMEM((STAGES, NC, 2, ROWS, hidden), BF16),
            pltpu.VMEM((STAGES, NC, 2, ROWS, hidden), BF16),
            pltpu.VMEM((STAGES, 4, NY, ROWS, width), F32),
            pltpu.VMEM((STAGES, 4 * NY, ROWS, width), BF16),
            pltpu.VMEM((STAGES, 4 * NY, ROWS, width), BF16),
            pltpu.VMEM((16, ROWS, width), BF16),
            pltpu.VMEM((16, ROWS, width), BF16),
            dma((7,)),
            gather_sems,
            gather_sems,
        ]
        + [dma(shape) for shape in pairs for _ in range(2)],
        compiler_params=pltpu.CompilerParams(collective_id=0, has_side_effects=True, vmem_limit_bytes=60 << 20),
    )(out_grad, inputs, preact.reshape(2, NY, ROWS, hidden), w_in, w_out)


def solution(mesh):
    placed = (
        P("wide", "col"),
        P("wide", "col"),
        P("col", "wide"),
        P("col", "wide"),
        P("wide", "col"),
    )
    return jax.shard_map(
        body,
        mesh=mesh,
        in_specs=placed,
        out_specs=(P("wide", "col"), P("col", "wide"), P("wide", "col")),
        check_vma=False,
    )
```

time: 86.1 us -> 82.5 us (0.958)
  the two profiles are of different devices: /device:TPU:40 before, /device:TPU:1 now
where the time goes in v2:
time: 82.5 us; the launch traced here: 82.4 us
  Pallas kernels  79.1 us (96%)
  local copies, waits for them, and re-layouts  2.64 us (3%)
    pallas_call x1, Pallas kernels, body(): pl.pallas_call(kernel, name='mlp_backward', out_shape=(pltpu.VMEM((ROWS,...  79.1 us
    unnamed x3, local copies, waits for them, and re-layouts  2.64 us

profile of v2, /device:TPU:1, one launch (start us, length us, event | category | flops | bytes accessed | tf_op | source)
XLA Modules:
  0.0 82.4 jit_solution(17014679509548063113)
XLA Ops:
  0.6 79.1 %mlp_backward.1 = (bf16[16,768]{1,0:T(8,128)(2,1)S(1)}, f32[768,384]{1,0:T(8,128)S(1)}, f32[384,768]{1,0:T(8,128)S(1)}) custom-call(bf16[16,768]{1,0:T(8,128)(2,1)} %grad_hbm.1, bf16[16,768]{1,0:T(8,128)(2,1)} %inp_hbm.1, bf16[2,4,16,384]{3,2,1,0:T(8,128)(2,1)} %bitcast.1, bf16[768,384]{1,0:T(8,128)(2,1)} %w_in_hbm.1, bf16[384,768]{1,0:T(8,128)(2,1)} %w_out_hbm.1), custom_call_target="tpu_custom_call" | custom-call | tf_op jit(solution)/shard_map/mlp_backward/pallas_call | solution.py:316
  79.8 0.6 copy.11
  80.4 1.0 %copy.12 = f32[768,384]{1,0:T(8,128)} copy(f32[768,384]{1,0:T(8,128)S(1)} %get-tuple-element.4) | data formatting | bytes 2359296
  81.4 1.0 %copy.13 = f32[384,768]{1,0:T(8,128)} copy(f32[384,768]{1,0:T(8,128)S(1)} %get-tuple-element.5) | data formatting | bytes 2359296

commit v3 on v2

--- a/solution.py
+++ b/solution.py
@@ -12,7 +12,7 @@
 NZ, NY, NC = 16, 4, 8
 ROWS = 16
 HEAD = 256
-INP_HEAD = 256
+INP_HEAD = 384
 INP_REACH = 2
 STAGES = 4
 BF16, F32 = jnp.bfloat16, jnp.float32
@@ -287,12 +287,12 @@
         wig[:INP_HEAD] = dot(flat(ia), flat(hid), ((0,), (0,)))
 
     for step, *index in (
-        (grad_rest, 1), (grad_head, 0), (wait_weights,), (start_inputs,), (grad_rest, 2), (grad_head, 1),
-        (inp_rest, 1), (inp_head, 0), (phase_b, 0), (wait_preact,), (gelu_part, 0), (gelu_part, 1), (grad_rest, 3),
-        (grad_head, 2), (inp_rest, 2), (inp_head, 1), (phase_b, 1), (phase_c, 0), (gelu_part, 2), (gelu_part, 3),
-        (grad_rest, 4), (grad_head, 3), (inp_rest, 3), (inp_head, 2), (phase_b, 2), (phase_c, 1), (phase_d, 0),
-        (grad_head, 4), (phase_b, 3), (inp_rest, 4), (inp_head, 3), (phase_c, 2), (phase_d, 1), (phase_e, 0),
-        (w_out_grad,), (phase_c, 3), (inp_head, 4), (phase_d, 2), (phase_e, 1), (phase_d, 3), (phase_e, 2),
+        (grad_rest, 1), (grad_head, 0), (wait_weights,), (grad_rest, 2), (grad_head, 1), (start_inputs,),
+        (phase_b, 0), (wait_preact,), (gelu_part, 0), (gelu_part, 1), (grad_rest, 3), (grad_head, 2), (phase_b, 1),
+        (phase_c, 0), (inp_rest, 1), (inp_head, 0), (gelu_part, 2), (gelu_part, 3), (grad_rest, 4), (grad_head, 3),
+        (phase_b, 2), (phase_c, 1), (phase_d, 0), (inp_rest, 2), (inp_head, 1), (grad_head, 4), (phase_b, 3),
+        (phase_c, 2), (phase_d, 1), (phase_e, 0), (inp_rest, 3), (inp_head, 2), (w_out_grad,), (phase_c, 3),
+        (phase_d, 2), (phase_e, 1), (inp_rest, 4), (inp_head, 3), (phase_d, 3), (phase_e, 2), (inp_head, 4),
         (phase_e, 3), (w_in_grad,),
     ):
         step(*index)

time: 82.5 us -> 79 us (0.958)
  Pallas kernels: 79.1 us -> 74.9 us
    pallas_call x1, Pallas kernels: 79.1 us -> 74.9 us  [body(): pl.pallas_call(kernel, name='mlp_backward', out_shape=(pltpu.VMEM((ROWS,...]
where the time goes in v3:
time: 79 us; the launch traced here: 78.1 us
  Pallas kernels  74.9 us (95%)
  local copies, waits for them, and re-layouts  2.64 us (3%)
    pallas_call x1, Pallas kernels, body(): pl.pallas_call(kernel, name='mlp_backward', out_shape=(pltpu.VMEM((ROWS,...  74.9 us
    unnamed x3, local copies, waits for them, and re-layouts  2.64 us

profile of v3, /device:TPU:1, one launch (start us, length us, event | category | flops | bytes accessed | tf_op | source)
XLA Modules:
  0.0 78.1 jit_solution(16912630940195580789)
XLA Ops:
  0.6 74.9 %mlp_backward.1 = (bf16[16,768]{1,0:T(8,128)(2,1)S(1)}, f32[768,384]{1,0:T(8,128)S(1)}, f32[384,768]{1,0:T(8,128)S(1)}) custom-call(bf16[16,768]{1,0:T(8,128)(2,1)} %grad_hbm.1, bf16[16,768]{1,0:T(8,128)(2,1)} %inp_hbm.1, bf16[2,4,16,384]{3,2,1,0:T(8,128)(2,1)} %bitcast.1, bf16[768,384]{1,0:T(8,128)(2,1)} %w_in_hbm.1, bf16[384,768]{1,0:T(8,128)(2,1)} %w_out_hbm.1), custom_call_target="tpu_custom_call" | custom-call | tf_op jit(solution)/shard_map/mlp_backward/pallas_call | solution.py:316
  75.5 0.6 copy.11
  76.1 1.0 %copy.12 = f32[768,384]{1,0:T(8,128)} copy(f32[768,384]{1,0:T(8,128)S(1)} %get-tuple-element.4) | data formatting | bytes 2359296
  77.1 1.0 %copy.13 = f32[384,768]{1,0:T(8,128)} copy(f32[384,768]{1,0:T(8,128)S(1)} %get-tuple-element.5) | data formatting | bytes 2359296

commit v4 on v3

--- a/solution.py
+++ b/solution.py
@@ -129,7 +129,7 @@
 
         def y_pass(offset):
             block = rest.at[at_z(offset), y]
-            for d in (1, 3, 2):
+            for d in (2, 1, 3):
                 slot = NY * slot_of(offset) + d
                 send(block, block, ry_s.at[slot], ry_r.at[slot], dev_y(d))
 
@@ -165,7 +165,7 @@
             if rest is not None:
                 z_start(rest_block)
             block = head.at[z, y]
-            for d in (1, 3, 2):
+            for d in (2, 1, 3):
                 send(block, block, hy_s.at[d], hy_r.at[d], dev_y(d))
             if rest is not None:
                 y_pass(0)
@@ -240,7 +240,7 @@
         for quarter in (3, 0, 2, 1):
             offset = stage_offset(stage, quarter)
             total = part[stage, quarter, y]
-            for d in (1, 3, 2):
+            for d in (2, 1, 3):
                 slot = NY * quarter + d
                 arrived(yr.at[stage, slot], y_s.at[stage, slot], y_r.at[stage, slot])
                 total = total + yr[stage, slot].astype(F32)

time: 79 us -> 78.8 us (level)
  no operation moved by 1% of the time
where the time goes in v4:
time: 78.8 us; the launch traced here: 78.6 us
  Pallas kernels  75.4 us (96%)
  local copies, waits for them, and re-layouts  2.64 us (3%)
    pallas_call x1, Pallas kernels, body(): pl.pallas_call(kernel, name='mlp_backward', out_shape=(pltpu.VMEM((ROWS,...  75.4 us
    unnamed x3, local copies, waits for them, and re-layouts  2.64 us

profile of v4, /device:TPU:1, one launch (start us, length us, event | category | flops | bytes accessed | tf_op | source)
XLA Modules:
  0.0 78.6 jit_solution(3369014042417394833)
XLA Ops:
  0.6 75.4 %mlp_backward.1 = (bf16[16,768]{1,0:T(8,128)(2,1)S(1)}, f32[768,384]{1,0:T(8,128)S(1)}, f32[384,768]{1,0:T(8,128)S(1)}) custom-call(bf16[16,768]{1,0:T(8,128)(2,1)} %grad_hbm.1, bf16[16,768]{1,0:T(8,128)(2,1)} %inp_hbm.1, bf16[2,4,16,384]{3,2,1,0:T(8,128)(2,1)} %bitcast.1, bf16[768,384]{1,0:T(8,128)(2,1)} %w_in_hbm.1, bf16[384,768]{1,0:T(8,128)(2,1)} %w_out_hbm.1), custom_call_target="tpu_custom_call" | custom-call | tf_op jit(solution)/shard_map/mlp_backward/pallas_call | solution.py:316
  76.0 0.6 copy.11
  76.6 1.0 %copy.12 = f32[768,384]{1,0:T(8,128)} copy(f32[768,384]{1,0:T(8,128)S(1)} %get-tuple-element.4) | data formatting | bytes 2359296
  77.6 1.0 %copy.13 = f32[384,768]{1,0:T(8,128)} copy(f32[384,768]{1,0:T(8,128)S(1)} %get-tuple-element.5) | data formatting | bytes 2359296
